TPU v7x, 32 devices: a whole 2x2x4 slice. The times are simulated.
32 devices in a mesh: partner: 8 (over y, x, core), blk: 4 (over z).
Axes of the slice: x: 2, y: 2, z: 4, core: 2. Of those that a mesh axis runs over, the one named last changes fastest.
Arguments:
- tensor_slab: float32 [8, 8192, 2048], P(None, 'partner', 'blk'), may hold values from -6 to 6
- sign_flips: int32 [8192], P('partner'), may hold values from -1 to 1, as said below
- mode2_factor: float32 [2048, 64], P('blk'), may hold values from -6 to 6
- mode3_factor: float32 [8, 64], replicated, may hold values from -6 to 6
- fibre_col: int32 [2048], P('blk'), may hold values from 0 to 511
- fibre_depth: int32 [2048], P('blk'), may hold values from 0 to 7
Outputs:
- mixed_slab: float32 [8, 8192, 2048], P(None, 'partner', 'blk')
- factor_update: float32 [8192, 64], P('partner')
Inputs may be any that keep to these rules, and one draw needn't show every extreme that they name: `sign_flips`: every entry is -1 or 1.
All inputs are finite; a program needn't handle non-finite values.
Results may differ from a plain program's by a relative error of at most 0.000098.
Values sent between devices are 32-bit elements; how exact they have to be, the bound alone decides.
A program may use at most 128 MiB of HBM per device.

v0:
```python
import math

import jax
import jax.numpy as jnp
from jax import lax
from jax.sharding import PartitionSpec as P

ridge = 0.1


def swapped(value, axis, stride):
    mask = 2**stride
    pairs = [(source, source ^ mask) for source in range(lax.axis_size(axis))]
    return lax.ppermute(value, axis, pairs)


def hadamard_table(order_len):
    rows_idx = lax.broadcasted_iota(jnp.int32, (order_len, order_len), 0)
    cols_idx = lax.broadcasted_iota(jnp.int32, (order_len, order_len), 1)
    common = jnp.bitwise_and(rows_idx, cols_idx)
    parity = jnp.zeros((order_len, order_len), jnp.int32)
    for bit_place in range(order_len.bit_length() - 1):
        parity = parity + jnp.bitwise_and(jnp.right_shift(common, bit_place), 1)
    return (1 - 2 * jnp.bitwise_and(parity, 1)).astype(jnp.float32)


def solve_normal(gram, moment):
    factor_chol = jnp.linalg.cholesky(gram)
    return jax.scipy.linalg.cho_solve((factor_chol, True), moment.T).T


def contract_samples(picked, khatri):
    return lax.dot_general(
        picked, khatri, (((0,), (0,)), ((), ())), precision=lax.Precision.HIGHEST
    )


def shards(tensor_slab, sign_flips, mode2_factor, mode3_factor, fibre_col, fibre_depth):
    flipped = tensor_slab * sign_flips.astype(jnp.float32)[None, :, None]
    depth_count, local_rows, block_cols = flipped.shape
    parties = lax.axis_size("partner")
    mixed = jnp.einsum(
        "ab,kbj->kaj", hadamard_table(local_rows), flipped, precision=lax.Precision.HIGHEST
    )
    my_index = lax.axis_index("partner")
    for bit_place in range(parties.bit_length() - 1):
        other_half = swapped(mixed, "partner", bit_place)
        upper_side = jnp.bitwise_and(jnp.right_shift(my_index, bit_place), 1) == 1
        mixed = jnp.where(upper_side, other_half - mixed, mixed + other_half)
    mixed_slab = mixed * (1.0 / math.sqrt(local_rows * parties))
    total_count = fibre_col.shape[0] * lax.axis_size("blk")
    picked = mixed_slab[fibre_depth, :, fibre_col]
    khatri = mode2_factor[fibre_col] * mode3_factor[fibre_depth]
    moment_scale = 1.0 / math.sqrt(total_count)
    gram_part = contract_samples(khatri, khatri) * (1.0 / total_count)
    identity = jnp.eye(khatri.shape[1], dtype=jnp.float32)
    moment_part = contract_samples(picked, khatri) * moment_scale
    moment, gram = lax.psum((moment_part, gram_part), "blk")
    factor_update = solve_normal(gram + ridge * identity, moment)
    return (mixed_slab, factor_update)


def solution(mesh):
    return jax.shard_map(
        shards,
        mesh=mesh,
        in_specs=(P(None, "partner", "blk"), P("partner"), P("blk", None), P(), P("blk"), P("blk")),
        out_specs=(P(None, "partner", "blk"), P("partner", None)),
        check_vma=False,
    )
```

profile of v0, /device:TPU:0, one launch (start us, length us, event | category | flops | bytes accessed | tf_op | source)
XLA Modules:
  0.0 988.5 jit_solution(17590509183416573934)
XLA Ops:
  7.2 0.0 copy-start
  7.2 0.0 copy-start.2
  7.2 0.0 all-reduce.2.cloned.1.call-start
  7.2 4.7 fusion.80
  11.9 0.0 copy-done.2
  11.9 112.2 %fusion.2 = f32[8,1024,512]{1,2,0:T(8,128)} fusion(f32[8,1024,512]{2,1,0:T(8,128)} %param.6, f32[1024]{0:T(1024)S(1)} %convert_element_type.7, f32[1024,1024,1]{1,0,2:T(8,128)S(1)} %fusion.80), kind=kOutput, calls=%fused_computation.8 | convolution fusion | flops 51543801856 | bytes 37752832 | tf_op jit(solution)/shard_map/ab,kbj->kaj/dot_general | solution.py:42
  124.2 0.5 collective-permute-start
  124.6 25.1 %collective-permute-done = f32[8,1024,512]{1,2,0:T(8,128)} collective-permute-done((f32[8,1024,512]{1,2,0:T(8,128)}, f32[8,1024,512]{1,2,0:T(8,128)}, u32[]{:S(2)}, u32[]{:S(2)}) %collective-permute-start) | collective-permute-done | bytes 16777248 | tf_op jit(solution)/shard_map/ppermute | solution.py:14
  149.7 17.3 %add_select_fusion.1 = f32[8,1024,512]{1,2,0:T(8,128)} fusion(f32[8,1024,512]{1,2,0:T(8,128)} %fusion.2, f32[8,1024,512]{1,2,0:T(8,128)} %collective-permute-done, pred[]{:T(512)S(6)} %eq.12), kind=kLoop, calls=%fused_computation.5 | loop fusion | flops 12582912 | bytes 50331648 | tf_op jit(solution)/shard_map/jit(_where)/select_n | solution.py:49
  167.0 2.9 collective-permute-start.1
  169.9 0.0 copy-start.1
  169.9 0.0 copy-start.3
  169.9 0.0 copy-start.4
  169.9 360.8 %collective-permute-done.1 = f32[8,1024,512]{1,2,0:T(8,128)} collective-permute-done((f32[8,1024,512]{1,2,0:T(8,128)}, f32[8,1024,512]{1,2,0:T(8,128)}, u32[]{:S(2)}, u32[]{:S(2)}) %collective-permute-start.1) | collective-permute-done | bytes 16777248 | tf_op jit(solution)/shard_map/ppermute | solution.py:14
  530.7 17.3 %add_select_fusion = f32[8,1024,512]{1,2,0:T(8,128)} fusion(f32[8,1024,512]{1,2,0:T(8,128)} %add_select_fusion.1, f32[8,1024,512]{1,2,0:T(8,128)} %collective-permute-done.1, pred[]{:T(512)S(6)} %eq.11), kind=kLoop, calls=%fused_computation.4 | loop fusion | flops 12582912 | bytes 50331648 | tf_op jit(solution)/shard_map/jit(_where)/select_n | solution.py:49
  548.0 1.8 collective-permute-start.2
  549.8 0.0 copy-done.1
  549.8 0.1 copy.9
  549.9 0.0 copy-done.3
  549.9 0.0 copy-done.4
  550.0 1.0 gather_fusion
  551.0 0.0 copy-done
  551.0 1.0 gather_fusion.1
  552.1 0.6 convolution_multiply_fusion.1
  552.7 19.3 %psum.14 = f32[64,64]{1,0:T(8,128)S(1)} all-reduce(f32[64,64]{1,0:T(8,128)S(1)} %convolution_multiply_fusion.1), channel_id=1, replica_groups=mesh['partner'=8,'blk'=4] {'blk'}, use_global_device_ids=true, to_apply=%region_0.1 | all-reduce | flops 4096 | bytes 32768 | tf_op jit(solution)/shard_map/psum | solution.py:58
  572.0 0.1 copy.10
  572.1 5.8 cholesky.16
  578.0 332.1 %collective-permute-done.2 = f32[8,1024,512]{1,2,0:T(8,128)} collective-permute-done((f32[8,1024,512]{1,2,0:T(8,128)}, f32[8,1024,512]{1,2,0:T(8,128)}, u32[]{:S(2)}, u32[]{:S(2)}) %collective-permute-start.2) | collective-permute-done | bytes 16777248 | tf_op jit(solution)/shard_map/ppermute | solution.py:14
  910.1 17.3 %select_multiply_fusion = f32[8,1024,512]{1,2,0:T(8,128)} fusion(f32[8,1024,512]{1,2,0:T(8,128)} %add_select_fusion, f32[8,1024,512]{1,2,0:T(8,128)} %collective-permute-done.2, pred[]{:T(512)S(6)} %eq.10), kind=kLoop, calls=%fused_computation.3 | loop fusion | flops 16777216 | bytes 50331648 | tf_op jit(solution)/shard_map/mul | solution.py:50
  927.4 7.5 gather_fusion.2
  934.9 4.3 convolution_multiply_fusion
  939.2 0.0 all-reduce.2.cloned.1.call-update
  939.2 0.6 compare_reduce_fusion
  939.9 0.7 fusion.55
  940.5 4.9 custom-call.10
  945.4 16.5 %copy.11 = f32[8,1024,512]{2,1,0:T(8,128)} copy(f32[8,1024,512]{1,2,0:T(8,128)} %select_multiply_fusion) | data formatting | bytes 33554432
  961.9 16.9 %all-reduce.2.cloned.1.call-done = f32[1024,64]{1,0:T(8,128)} async-done(((f32[1024,64]{1,0:T(8,128)}), f32[1024,64]{1,0:T(8,128)}) %all-reduce.2.cloned.1.call-update) | async-done | bytes 262160 | tf_op jit(solution)/shard_map/psum | solution.py:58
  978.9 1.8 fusion.58
  980.6 1.1 fusion.56
  (6 shorter events, 0.1 us)
Async XLA Ops:
  7.2 543.9 %copy-start = (f32[8,64]{1,0:T(8,128)S(1)}, f32[8,64]{1,0:T(8,128)}, u32[]{:S(2)}) copy-start(f32[8,64]{1,0:T(8,128)} %param.9) | copy-start | bytes 6148
  7.2 4.7 copy-start.2
  7.2 971.7 %all-reduce.2.cloned.1.call-start = ((), (), s32[]{:S(2)}) async-start(), calls=%async_computation | async-start | bytes 1048576 | tf_op jit(solution)/shard_map/psum | solution.py:58
  124.2 25.6 %collective-permute-start = (f32[8,1024,512]{1,2,0:T(8,128)}, f32[8,1024,512]{1,2,0:T(8,128)}, u32[]{:S(2)}, u32[]{:S(2)}) collective-permute-start(f32[8,1024,512]{1,2,0:T(8,128)} %fusion.2), channel_id=1, source_target_pairs={{0,4},{4,0},{8,12},{12,8},{16,20},{20,16},{24,28},{28,24},{1,5},{5... | collective-permute-start | bytes 50331656 | tf_op jit(solution)/shard_map/ppermute | solution.py:14
  167.0 363.7 %collective-permute-start.1 = (f32[8,1024,512]{1,2,0:T(8,128)}, f32[8,1024,512]{1,2,0:T(8,128)}, u32[]{:S(2)}, u32[]{:S(2)}) collective-permute-start(f32[8,1024,512]{1,2,0:T(8,128)} %add_select_fusion.1), channel_id=1, source_target_pairs={{0,8},{4,12},{8,0},{12,4},{16,24},{20,28},{24,16},{28,20},{1,9},{5... | collective-permute-start | bytes 50331656 | tf_op jit(solution)/shard_map/ppermute | solution.py:14
  169.9 379.9 %copy-start.1 = (f32[512,64]{0,1:T(8,128)S(1)}, f32[512,64]{0,1:T(8,128)}, u32[]{:S(2)}) copy-start(f32[512,64]{0,1:T(8,128)} %param.8) | copy-start | bytes 393220
  169.9 380.0 %copy-start.3 = (s32[512]{0:T(512)S(1)}, s32[512]{0:T(512)}, u32[]{:S(2)}) copy-start(s32[512]{0:T(512)} %param.11) | copy-start | bytes 6148
  169.9 380.0 %copy-start.4 = (s32[512]{0:T(512)S(1)}, s32[512]{0:T(512)}, u32[]{:S(2)}) copy-start(s32[512]{0:T(512)} %param.10) | copy-start | bytes 6148
  548.0 362.1 %collective-permute-start.2 = (f32[8,1024,512]{1,2,0:T(8,128)}, f32[8,1024,512]{1,2,0:T(8,128)}, u32[]{:S(2)}, u32[]{:S(2)}) collective-permute-start(f32[8,1024,512]{1,2,0:T(8,128)} %add_select_fusion), channel_id=1, source_target_pairs={{0,16},{4,20},{8,24},{12,28},{16,0},{20,4},{24,8},{28,12},{1,17},{... | collective-permute-start | bytes 50331656 | tf_op jit(solution)/shard_map/ppermute | solution.py:14
Sparse Core Ops, SparseCore 0:
  939.4 39.4 all-reduce.1
where the time goes:
time: 989 us
  waiting for transfers between devices  735 us (74%)
  matrix products  120 us (12%)
  other arithmetic  68.7 us (7%)
  local copies, waits for them, and re-layouts  26.3 us (3%)
  blocking collectives  19.3 us (2%)
  between operations  14.2 us (1%)
    ppermute x3, waiting for transfers between devices, swapped(): return lax.ppermute(value, axis, pairs)  718 us
    dot_general x1, matrix products, shards(): jnp.einsum('ab,kbj->kaj', hadamard_table(local_rows), flipped, precision=...  112 us
    select_n x2, other arithmetic, shards(): mixed = jnp.where(upper_side, other_half - mixed, mixed + other_half)  34.6 us
  transfers between devices with their start and end apart: 4, of which 4 were waited for; matrix products, arithmetic and copies ran while one was open for 3% of the time, Pallas kernels for 0%

commit v1 on v0

v1 whole, which is shorter than its diff:
```python
import functools
import math

import jax
import jax.numpy as jnp
from jax import lax
from jax.experimental import pallas as pl
from jax.experimental.pallas import tpu as pltpu
from jax.sharding import PartitionSpec as P

ridge = 0.1
MESH = pl.DeviceIdType.MESH
f32 = jnp.float32
bf16 = jnp.bfloat16


def solve_normal(gram, moment):
    factor_chol = jnp.linalg.cholesky(gram)
    return jax.scipy.linalg.cho_solve((factor_chol, True), moment.T).T


def contract_samples(picked, khatri):
    return lax.dot_general(
        picked, khatri, (((0,), (0,)), ((), ())), precision=lax.Precision.HIGHEST
    )


def walsh_tile(order):
    rows_idx = lax.broadcasted_iota(jnp.int32, (order, order), 0)
    cols_idx = lax.broadcasted_iota(jnp.int32, (order, order), 1)
    parity = jnp.bitwise_and(rows_idx, cols_idx)
    shift = order.bit_length() - 1
    while shift > 1:
        shift = (shift + 1) // 2
        parity = jnp.bitwise_xor(parity, jnp.right_shift(parity, shift))
    return (1 - 2 * jnp.bitwise_and(parity, 1)).astype(f32)


def butterflies(parts):
    stride = 1
    while stride < len(parts):
        parts = [
            parts[at] + parts[at + stride] if at & stride == 0 else parts[at - stride] - parts[at]
            for at in range(len(parts))
        ]
        stride *= 2
    return parts


def split_two(value):
    high = value.astype(bf16)
    return high, (value - high.astype(f32)).astype(bf16)


def mixing_kernel(plan, slab, signs, out, held, landed, core_landed, near_signs, tables,
                  load_sem, link_send, link_recv, core_send, core_recv, sign_send, sign_recv, out_sem):
    parties, links, per_group, depth, slots = plan
    slices, rows, cols = held.shape
    tile = tables.shape[-1]
    blocks = rows // tile
    me = lax.axis_index("partner")

    def peer(bit):
        return jnp.bitwise_xor(me, 1 << bit)

    def side(bit):
        return (1 - 2 * jnp.bitwise_and(jnp.right_shift(me, bit), 1)).astype(f32)

    barrier = pltpu.get_barrier_semaphore()
    for bit in range(links + 1):
        pl.semaphore_signal(barrier, inc=1, device_id={"partner": peer(bit)}, device_id_type=MESH)
    pl.semaphore_wait(barrier, links + 1)

    total = links * per_group

    def chunk_at(link, slot):
        phase, turn = divmod(slot, per_group)
        chunk = (link - phase) % links + links * turn
        return chunk if chunk < slices else None

    def link_copy(link, slot):
        chunk = chunk_at(link, slot)
        if chunk is None:
            return None
        source = slab if slot < per_group else held
        return pltpu.make_async_remote_copy(
            src_ref=source.at[chunk],
            dst_ref=landed.at[link, slot % slots],
            send_sem=link_send.at[link, slot % slots],
            recv_sem=link_recv.at[link, slot % slots],
            device_id={"partner": peer(link + 1)},
            device_id_type=MESH,
        )

    def core_copy(link, slot):
        chunk = chunk_at(link, slot)
        if chunk is None:
            return None
        return pltpu.make_async_remote_copy(
            src_ref=held.at[chunk],
            dst_ref=core_landed.at[link, slot % 2],
            send_sem=core_send.at[link, slot % 2],
            recv_sem=core_recv.at[link, slot % 2],
            device_id={"partner": peer(0)},
            device_id_type=MESH,
        )

    def sign_copy(link):
        return pltpu.make_async_remote_copy(
            src_ref=signs,
            dst_ref=near_signs.at[link],
            send_sem=sign_send.at[link],
            recv_sem=sign_recv.at[link],
            device_id={"partner": peer(link + 1)},
            device_id_type=MESH,
        )

    def load_copy(chunk):
        return pltpu.make_async_copy(slab.at[chunk], held.at[chunk], load_sem.at[chunk])

    def out_copy(chunk):
        return pltpu.make_async_copy(held.at[chunk], out.at[chunk], out_sem.at[chunk])

    def combine(chunk, other, bit, scale):
        mine = side(bit) * scale
        step = min(rows, 64)

        @pl.loop(0, rows // step)
        def _(at):
            span = pl.ds(pl.multiple_of(at * step, step), step)
            held[chunk, span, :] = held[chunk, span, :] * mine + other[span, :] * scale

    for link in range(links):
        sign_copy(link).start()
    for slot in range(depth):
        for link in range(links):
            copy = link_copy(link, slot)
            if copy is not None:
                copy.start()
    for chunk in range(slices):
        load_copy(chunk).start()

    for link in range(links):
        sign_copy(link).wait()
    own_table = walsh_tile(tile)
    for link in range(links):
        for block in range(blocks):
            span = slice(block * tile, (block + 1) * tile)
            tables[link, 0, block] = (own_table * (signs[0:1, span] * side(link + 1))).astype(bf16)
            tables[link, 1, block] = (own_table * near_signs[link, 0:1, span]).astype(bf16)
    for chunk in range(slices):
        load_copy(chunk).wait()

    def transform(slot):
        count = min(links, slices - links * slot)
        width = min(cols, 256)
        tiles = cols // width

        @pl.loop(0, count * tiles)
        def _(at):
            link = at // tiles
            span = pl.ds(pl.multiple_of((at % tiles) * width, width), width)
            chunk = link + links * slot
            parts = []
            for block in range(blocks):
                lines = slice(block * tile, (block + 1) * tile)
                own_high, own_low = split_two(held[chunk, lines, span])
                far_high, far_low = split_two(landed[link, slot % slots, lines, span])
                own, far = tables[link, 0, block], tables[link, 1, block]
                sums = jnp.dot(own, own_high, preferred_element_type=f32)
                sums += jnp.dot(own, own_low, preferred_element_type=f32)
                sums += jnp.dot(far, far_high, preferred_element_type=f32)
                sums += jnp.dot(far, far_low, preferred_element_type=f32)
                parts.append(sums)
            for block, part in enumerate(butterflies(parts)):
                held[chunk, block * tile:(block + 1) * tile, span] = part

    scale = 1.0 / math.sqrt(rows * parties)
    for slot in range(total):
        if 1 <= slot <= per_group:
            for link in range(links):
                copy = core_copy(link, slot - 1)
                if copy is not None:
                    copy.wait()
                    combine(chunk_at(link, slot - 1), core_landed.at[link, (slot - 1) % 2], 0, 1.0)
        if slot < per_group:
            for link in range(links):
                copy = link_copy(link, slot)
                if copy is not None:
                    copy.wait()
            transform(slot)
            for link in range(links):
                copy = core_copy(link, slot)
                if copy is not None:
                    copy.start()
        else:
            last = slot >= total - per_group
            for link in range(links):
                copy = link_copy(link, slot)
                if copy is not None:
                    copy.wait()
                    chunk = chunk_at(link, slot)
                    combine(chunk, landed.at[link, slot % slots], link + 1, scale if last else 1.0)
                    if last:
                        out_copy(chunk).start()
        if slot + depth < total:
            for link in range(links):
                copy = link_copy(link, slot + depth)
                if copy is not None:
                    copy.start()
    for chunk in range(slices):
        out_copy(chunk).wait()


def mix(slab, sign_flips):
    slices, rows, cols = slab.shape
    parties = lax.axis_size("partner")
    links = parties.bit_length() - 2
    per_group = -(-slices // links)
    depth = 2
    total = links * per_group
    slots = 4 if slices % links == 0 else total
    tile = min(256, rows)
    blocks = rows // tile
    signs = jnp.broadcast_to(sign_flips.astype(f32)[None, :], (8, rows))
    plan = (parties, links, per_group, depth, slots)
    return pl.pallas_call(
        functools.partial(mixing_kernel, plan),
        out_shape=jax.ShapeDtypeStruct(slab.shape, f32),
        in_specs=[
            pl.BlockSpec(memory_space=pl.ANY),
            pl.BlockSpec(memory_space=pltpu.VMEM),
        ],
        out_specs=pl.BlockSpec(memory_space=pl.ANY),
        scratch_shapes=[
            pltpu.VMEM((slices, rows, cols), f32),
            pltpu.VMEM((links, slots, rows, cols), f32),
            pltpu.VMEM((links, 2, rows, cols), f32),
            pltpu.VMEM((links, 8, rows), f32),
            pltpu.VMEM((links, 2, blocks, tile, tile), bf16),
            pltpu.SemaphoreType.DMA((slices,)),
            pltpu.SemaphoreType.DMA((links, slots)),
            pltpu.SemaphoreType.DMA((links, slots)),
            pltpu.SemaphoreType.DMA((links, 2)),
            pltpu.SemaphoreType.DMA((links, 2)),
            pltpu.SemaphoreType.DMA((links,)),
            pltpu.SemaphoreType.DMA((links,)),
            pltpu.SemaphoreType.DMA((slices,)),
        ],
        compiler_params=pltpu.CompilerParams(
            collective_id=0, has_side_effects=True, vmem_limit_bytes=56 * 2**20
        ),
    )(slab, signs)


def shards(tensor_slab, sign_flips, mode2_factor, mode3_factor, fibre_col, fibre_depth):
    mixed_slab = mix(tensor_slab, sign_flips)
    total_count = fibre_col.shape[0] * lax.axis_size("blk")
    picked = mixed_slab[fibre_depth, :, fibre_col]
    khatri = mode2_factor[fibre_col] * mode3_factor[fibre_depth]
    moment_scale = 1.0 / math.sqrt(total_count)
    gram_part = contract_samples(khatri, khatri) * (1.0 / total_count)
    identity = jnp.eye(khatri.shape[1], dtype=jnp.float32)
    moment_part = contract_samples(picked, khatri) * moment_scale
    moment, gram = lax.psum((moment_part, gram_part), "blk")
    factor_update = solve_normal(gram + ridge * identity, moment)
    return (mixed_slab, factor_update)


def solution(mesh):
    return jax.shard_map(
        shards,
        mesh=mesh,
        in_specs=(P(None, "partner", "blk"), P("partner"), P("blk", None), P(), P("blk"), P("blk")),
        out_specs=(P(None, "partner", "blk"), P("partner", None)),
        check_vma=False,
    )
```

time: 989 us -> 470 us (0.48)
  waiting for transfers between devices: 735 us -> 6.97 us
  Pallas kernels: 0 us -> 369 us
  matrix products: 120 us -> 7.72 us
  other arithmetic: 68.7 us -> 12.8 us
  local copies, waits for them, and re-layouts: 26.3 us -> 39.9 us
    ppermute x3 -> x0, waiting for transfers between devices: 718 us -> none  [swapped(): return lax.ppermute(value, axis, pairs)]
    pallas_call x0 -> x1, Pallas kernels: none -> 369 us  [mix(): pl.pallas_call(functools.partial(mixing_kernel, plan), out_shape=jax.Shap...]
    dot_general x1 -> x0, matrix products: 112 us -> none  [shards(): jnp.einsum('ab,kbj->kaj', hadamard_table(local_rows), flipped, precision=...]
    select_n x2 -> x0, other arithmetic: 34.6 us -> none  [shards(): mixed = jnp.where(upper_side, other_half - mixed, mixed + other_half)]
    mul x1 -> x0, other arithmetic: 17.3 us -> none  [shards(): mixed_slab = mixed * (1.0 / math.sqrt(local_rows * parties))]
    pallas_call x0 -> x1, local copies, waits for them, and re-layouts: none -> 16.4 us  [mix(): pl.pallas_call(functools.partial(mixing_kernel, plan), out_shape=jax.Shap...]
    psum x1, waiting for transfers between devices: 16.9 us -> 6.95 us  [shards(): moment, gram = lax.psum((moment_part, gram_part), 'blk')]
  transfers between devices with their start and end apart: 4 -> 1, of which waited for: 4 -> 1; matrix products, arithmetic and copies ran while one was open for 3% -> 3% of each run, Pallas kernels for 0% -> 0%
where the time goes in v1:
time: 470 us
  Pallas kernels  369 us (79%)
  local copies, waits for them, and re-layouts  39.9 us (8%)
  blocking collectives  19.5 us (4%)
  between operations  14.2 us (3%)
  other arithmetic  12.8 us (3%)
  matrix products  7.72 us (2%)
  waiting for transfers between devices  6.97 us (1%)
    pallas_call x1, Pallas kernels, mix(): pl.pallas_call(functools.partial(mixing_kernel, plan), out_shape=jax.Shap...  369 us
    psum x1, blocking collectives, shards(): moment, gram = lax.psum((moment_part, gram_part), 'blk')  19.5 us
    pallas_call x1, local copies, waits for them, and re-layouts, mix(): pl.pallas_call(functools.partial(mixing_kernel, plan), out_shape=jax.Shap...  16.4 us
    unnamed x10, local copies, waits for them, and re-layouts  12.8 us
  transfers between devices with their start and end apart: 1, of which 1 were waited for; matrix products, arithmetic and copies ran while one was open for 3% of the time, Pallas kernels for 0%

profile of v1, /device:TPU:0, one launch (start us, length us, event | category | flops | bytes accessed | tf_op | source)
XLA Modules:
  0.0 469.7 jit_solution(196732846547217937)
XLA Ops:
  7.2 0.0 copy-start
  7.2 0.0 all-reduce.2.cloned.1.call-start
  7.2 1.0 copy.8
  8.3 0.7 convert_element_type.4
  9.0 0.6 broadcast_in_dim.7.signs
  9.6 368.6 %shard_map.77 = f32[8,1024,512]{2,1,0:T(8,128)} custom-call(f32[8,1024,512]{2,1,0:T(8,128)} %slab.1, f32[8,1024]{1,0:T(8,128)} %broadcast_in_dim.7.signs), custom_call_target="tpu_custom_call" | custom-call | tf_op jit(solution)/shard_map/pallas_call | solution.py:227
  378.2 0.0 copy-start.2
  378.2 0.0 copy-start.3
  378.2 16.4 %copy.10 = f32[8,1024,512]{1,2,0:T(8,128)} copy(f32[8,1024,512]{2,1,0:T(8,128)} %shard_map.77) | data formatting | bytes 33554432 | tf_op jit(solution)/shard_map/pallas_call | solution.py:227
  394.6 0.0 copy-done.2
  394.6 0.0 copy-done.3
  394.6 1.0 gather_fusion
  395.6 0.0 copy-done
  395.6 1.0 gather_fusion.1
  396.7 7.9 %gather_fusion.2 = f32[512,1024]{1,0:T(8,128)S(1)} fusion(f32[8,1024,512]{1,2,0:T(8,128)} %copy.10, s32[512]{0:T(512)S(1)} %get-tuple-element.3), kind=kCustom, calls=%fused_computation.2 | custom fusion | bytes 4198400 | tf_op jit(solution)/shard_map/gather | solution.py:259
  404.6 4.3 convolution_multiply_fusion
  408.9 0.0 all-reduce.2.cloned.1.call-update
  409.0 0.6 convolution_multiply_fusion.1
  409.6 19.5 %psum.14 = f32[64,64]{1,0:T(8,128)S(1)} all-reduce(f32[64,64]{1,0:T(8,128)S(1)} %convolution_multiply_fusion.1), channel_id=1, replica_groups=mesh['partner'=8,'blk'=4] {'blk'}, use_global_device_ids=true, to_apply=%region_0.0 | all-reduce | flops 4096 | bytes 32768 | tf_op jit(solution)/shard_map/psum | solution.py:265
  429.1 0.1 copy.9
  429.2 5.8 %cholesky.16 = f32[64,64]{1,0:T(8,128)S(1)} custom-call(f32[64,64]{1,0:T(8,128)S(1)} %fusion.7), custom_call_target="Cholesky" | custom-call | tf_op jit(solution)/shard_map/jit(cholesky)/cholesky | solution.py:18
  435.1 0.6 compare_reduce_fusion
  435.7 0.7 fusion.2
  436.4 4.9 %custom-call.10 = f32[1,64,64]{1,2,0:T(8,128)S(1)} custom-call(f32[1,64,64]{2,1,0:T(8,128)S(1)} %fusion.2), custom_call_target="InvertDiagBlocksLowerTriangular" | custom-call | tf_op jit(solution)/shard_map/jit(_cho_solve)/triangular_solve | solution.py:19
  441.3 6.9 %all-reduce.2.cloned.1.call-done = f32[1024,64]{1,0:T(8,128)} async-done(((f32[1024,64]{1,0:T(8,128)}), f32[1024,64]{1,0:T(8,128)}) %all-reduce.2.cloned.1.call-update) | async-done | bytes 262160 | tf_op jit(solution)/shard_map/psum | solution.py:265
  448.2 1.7 fusion.5
  450.0 1.1 fusion.3
  451.1 0.0 copy-start.1
  451.1 11.8 %copy.13 = f32[8,1024,512]{2,1,0:T(8,128)} copy(f32[8,1024,512]{2,1,0:T(8,128)} %shard_map.77) | data formatting | bytes 33554432
  462.8 0.0 copy-done.1
  (5 shorter events, 0.1 us)
Async XLA Ops:
  7.2 388.5 %copy-start = (f32[8,64]{1,0:T(8,128)S(1)}, f32[8,64]{1,0:T(8,128)}, u32[]{:S(2)}) copy-start(f32[8,64]{1,0:T(8,128)} %param.9) | copy-start | bytes 6148
  7.2 441.0 %all-reduce.2.cloned.1.call-start = ((), (), s32[]{:S(2)}) async-start(), calls=%async_computation | async-start | bytes 1048576 | tf_op jit(solution)/shard_map/psum | solution.py:265
  378.2 16.4 %copy-start.2 = (s32[512]{0:T(512)S(1)}, s32[512]{0:T(512)}, u32[]{:S(2)}) copy-start(s32[512]{0:T(512)} %param.11) | copy-start | bytes 6148
  378.2 16.4 %copy-start.3 = (s32[512]{0:T(512)S(1)}, s32[512]{0:T(512)}, u32[]{:S(2)}) copy-start(s32[512]{0:T(512)} %param.10) | copy-start | bytes 6148
  451.1 11.8 %copy-start.1 = (f32[8,64]{1,0:T(8,128)S(1)}, f32[8,64]{1,0:T(8,128)}, u32[]{:S(2)}) copy-start(f32[8,64]{1,0:T(8,128)} %param.9) | copy-start | bytes 6148
Sparse Core Ops, SparseCore 0:
  409.1 39.0 all-reduce.1

commit v2 on v1

--- a/solution.py
+++ b/solution.py
@@ -12,17 +12,6 @@
 MESH = pl.DeviceIdType.MESH
 f32 = jnp.float32
 bf16 = jnp.bfloat16
-
-
-def solve_normal(gram, moment):
-    factor_chol = jnp.linalg.cholesky(gram)
-    return jax.scipy.linalg.cho_solve((factor_chol, True), moment.T).T
-
-
-def contract_samples(picked, khatri):
-    return lax.dot_general(
-        picked, khatri, (((0,), (0,)), ((), ())), precision=lax.Precision.HIGHEST
-    )
 
 
 def walsh_tile(order):
@@ -52,13 +41,43 @@
     return high, (value - high.astype(f32)).astype(bf16)
 
 
-def mixing_kernel(plan, slab, signs, out, held, landed, core_landed, near_signs, tables,
-                  load_sem, link_send, link_recv, core_send, core_recv, sign_send, sign_recv, out_sem):
-    parties, links, per_group, depth, slots = plan
+def exact_dot(left, right):
+    return jnp.dot(left, right, precision=lax.Precision.HIGHEST, preferred_element_type=f32)
+
+
+def inverse_of(gram):
+    order = gram.shape[0]
+    rows_idx = lax.broadcasted_iota(jnp.int32, (order, order), 0)
+    cols_idx = lax.broadcasted_iota(jnp.int32, (order, order), 1)
+
+    def eliminate(at, work):
+        on_row, on_col = rows_idx == at, cols_idx == at
+        row = jnp.sum(jnp.where(on_row, work, 0.0), axis=0, keepdims=True)
+        col = jnp.sum(jnp.where(on_col, work, 0.0), axis=1, keepdims=True)
+        pivot = jnp.sum(jnp.where(on_col[0:1], row, 0.0), axis=1, keepdims=True)
+        row = jnp.where(on_col[0:1], 1.0, row) / pivot
+        return jnp.where(on_row, row, jnp.where(on_col, 0.0, work) - col * row)
+
+    found = lax.fori_loop(0, order, eliminate, gram)
+    identity = (rows_idx == cols_idx).astype(f32)
+    return found + exact_dot(found, identity - exact_dot(gram, found))
+
+
+def mixing_kernel(plan, slab, flips, fibre_col, fibre_depth, mode2_wide, mode3, out, update_wide,
+                  held, landed, core_landed, signs, near_signs, tables,
+                  mode2, update, moment, gram, moment_in, gram_in, packed, packed_in, gathered,
+                  load_sem, link_send, link_recv, core_send, core_recv, sign_send, sign_recv, out_sem,
+                  moment_send, moment_recv, gram_send, gram_recv, pack_send, pack_recv, gather_send, gather_recv):
+    parties, blks, links, per_group, depth, slots = plan
     slices, rows, cols = held.shape
     tile = tables.shape[-1]
     blocks = rows // tile
     me = lax.axis_index("partner")
+    my_blk = lax.axis_index("blk")
+    share = rows // blks
+    rank = mode2.shape[1]
+    scale = 1.0 / math.sqrt(rows * parties)
+    sample_count = fibre_col.shape[1] * blks
 
     def peer(bit):
         return jnp.bitwise_xor(me, 1 << bit)
@@ -69,7 +88,9 @@
     barrier = pltpu.get_barrier_semaphore()
     for bit in range(links + 1):
         pl.semaphore_signal(barrier, inc=1, device_id={"partner": peer(bit)}, device_id_type=MESH)
-    pl.semaphore_wait(barrier, links + 1)
+    for off in range(1, blks):
+        pl.semaphore_signal(barrier, inc=1, device_id={"blk": lax.rem(my_blk + off, blks)}, device_id_type=MESH)
+    pl.semaphore_wait(barrier, links + blks)
 
     total = links * per_group
 
@@ -130,8 +151,6 @@
             span = pl.ds(pl.multiple_of(at * step, step), step)
             held[chunk, span, :] = held[chunk, span, :] * mine + other[span, :] * scale
 
-    for link in range(links):
-        sign_copy(link).start()
     for slot in range(depth):
         for link in range(links):
             copy = link_copy(link, slot)
@@ -139,6 +158,9 @@
                 copy.start()
     for chunk in range(slices):
         load_copy(chunk).start()
+    signs[...] = jnp.broadcast_to(flips[...].astype(f32), signs.shape)
+    for link in range(links):
+        sign_copy(link).start()
 
     for link in range(links):
         sign_copy(link).wait()
@@ -175,7 +197,125 @@
             for block, part in enumerate(butterflies(parts)):
                 held[chunk, block * tile:(block + 1) * tile, span] = part
 
-    scale = 1.0 / math.sqrt(rows * parties)
+    def rows_of(blk):
+        return pl.ds(pl.multiple_of(blk * share, share), share)
+
+    def moment_copy(off):
+        target = lax.rem(my_blk + off, blks)
+        return pltpu.make_async_remote_copy(
+            src_ref=moment.at[rows_of(target)],
+            dst_ref=moment_in.at[off - 1],
+            send_sem=moment_send.at[off - 1],
+            recv_sem=moment_recv.at[off - 1],
+            device_id={"blk": target},
+            device_id_type=MESH,
+        )
+
+    def gram_copy(off):
+        return pltpu.make_async_remote_copy(
+            src_ref=gram,
+            dst_ref=gram_in.at[off - 1],
+            send_sem=gram_send.at[off - 1],
+            recv_sem=gram_recv.at[off - 1],
+            device_id={"blk": lax.rem(my_blk + off, blks)},
+            device_id_type=MESH,
+        )
+
+    def pack_copy(bit):
+        return pltpu.make_async_remote_copy(
+            src_ref=packed.at[bit],
+            dst_ref=packed_in.at[bit],
+            send_sem=pack_send.at[bit],
+            recv_sem=pack_recv.at[bit],
+            device_id={"partner": peer(bit)},
+            device_id_type=MESH,
+        )
+
+    def gather_copy(off):
+        return pltpu.make_async_remote_copy(
+            src_ref=packed.at[links + 1],
+            dst_ref=gathered.at[off - 1],
+            send_sem=gather_send.at[off - 1],
+            recv_sem=gather_recv.at[off - 1],
+            device_id={"blk": lax.rem(my_blk + off, blks)},
+            device_id_type=MESH,
+        )
+
+    def contract_local():
+        mode2[...] = mode2_wide[...].T
+        moment[...] = jnp.zeros_like(moment)
+        gram[...] = jnp.zeros_like(gram)
+        samples = fibre_col.shape[1]
+
+        @pl.loop(0, slices)
+        def _(chunk):
+            place = lax.broadcasted_iota(jnp.int32, (cols, samples), 0) + chunk * cols
+            sampled = fibre_depth[...] * cols + fibre_col[...]
+            counts = jnp.sum((place == sampled).astype(f32), axis=1, keepdims=True)
+            khatri = mode2[...] * mode3[pl.ds(chunk, 1), :]
+            weights = khatri * counts
+            gram[...] += exact_dot(weights.T, khatri)
+
+            @pl.loop(0, blocks)
+            def _(block):
+                lines = pl.ds(pl.multiple_of(block * tile, tile), tile)
+                moment[lines, :] += exact_dot(held[chunk, lines, :], weights)
+
+        parts = []
+        for block in range(blocks):
+            value = moment[block * tile:(block + 1) * tile, :]
+            high, rest = split_two(value)
+            low = (value - high.astype(f32) - rest.astype(f32)).astype(bf16)
+            table = tables[0, 0, block]
+            sums = jnp.dot(table, low, preferred_element_type=f32)
+            sums += jnp.dot(table, rest, preferred_element_type=f32)
+            sums += jnp.dot(table, high, preferred_element_type=f32)
+            parts.append(sums * side(1))
+        for block, part in enumerate(butterflies(parts)):
+            moment[block * tile:(block + 1) * tile, :] = part
+        for off in range(1, blks):
+            moment_copy(off).start()
+            gram_copy(off).start()
+
+    def solve_share():
+        for off in range(1, blks):
+            moment_copy(off).wait()
+            gram_copy(off).wait()
+        whole_gram = gram[...]
+        own = moment[rows_of(my_blk), :]
+        for off in range(1, blks):
+            whole_gram = whole_gram + gram_in[off - 1]
+            own = own + moment_in[off - 1]
+        rows_idx = lax.broadcasted_iota(jnp.int32, (rank, rank), 0)
+        cols_idx = lax.broadcasted_iota(jnp.int32, (rank, rank), 1)
+        whole_gram = whole_gram * (1.0 / sample_count) + jnp.where(rows_idx == cols_idx, ridge, 0.0)
+        solved = exact_dot(own * (scale / math.sqrt(sample_count)), inverse_of(whole_gram))
+        packed[0] = jnp.concatenate([solved[: share // 2], solved[share // 2:]], axis=1)
+        pack_copy(0).start()
+
+    def pack_step(bit):
+        pack_copy(bit).wait()
+        packed[bit + 1] = packed[bit] * side(bit) + packed_in[bit]
+        if bit < links:
+            pack_copy(bit + 1).start()
+        else:
+            for off in range(1, blks):
+                gather_copy(off).start()
+
+    def write_share(blk, value):
+        half = share // 2
+        for at in range(2):
+            lines = pl.ds(pl.multiple_of(blk * share + at * half, half), half)
+            update[lines, :] = value[:, at * rank:(at + 1) * rank]
+
+    def write_update():
+        write_share(my_blk, packed[links + 1])
+        for off in range(1, blks):
+            gather_copy(off).wait()
+            write_share(lax.rem(my_blk + blks - off, blks), gathered[off - 1])
+        update_wide[...] = update[...].T
+
+    contract_local()
     for slot in range(total):
         if 1 <= slot <= per_group:
             for link in range(links):
@@ -208,13 +348,20 @@
                 copy = link_copy(link, slot + depth)
                 if copy is not None:
                     copy.start()
+        if slot == 1:
+            solve_share()
+        elif 2 <= slot <= links + 2:
+            pack_step(slot - 2)
+        elif slot == links + 3:
+            write_update()
     for chunk in range(slices):
         out_copy(chunk).wait()
 
 
-def mix(slab, sign_flips):
-    slices, rows, cols = slab.shape
-    parties = lax.axis_size("partner")
+def shards(tensor_slab, sign_flips, mode2_factor, mode3_factor, fibre_col, fibre_depth):
+    slices, rows, cols = tensor_slab.shape
+    rank = mode2_factor.shape[1]
+    parties, blks = lax.axis_size("partner"), lax.axis_size("blk")
     links = parties.bit_length() - 2
     per_group = -(-slices // links)
     depth = 2
@@ -222,49 +369,66 @@
     slots = 4 if slices % links == 0 else total
     tile = min(256, rows)
     blocks = rows // tile
-    signs = jnp.broadcast_to(sign_flips.astype(f32)[None, :], (8, rows))
-    plan = (parties, links, per_group, depth, slots)
-    return pl.pallas_call(
+    share = rows // blks
+    packed_shape = (share // 2, 2 * rank)
+    others = max(blks - 1, 1)
+    plan = (parties, blks, links, per_group, depth, slots)
+    dma = pltpu.SemaphoreType.DMA
+    vmem = pl.BlockSpec(memory_space=pltpu.VMEM)
+    anywhere = pl.BlockSpec(memory_space=pl.ANY)
+    mixed_slab, update_wide = pl.pallas_call(
         functools.partial(mixing_kernel, plan),
-        out_shape=jax.ShapeDtypeStruct(slab.shape, f32),
-        in_specs=[
-            pl.BlockSpec(memory_space=pl.ANY),
-            pl.BlockSpec(memory_space=pltpu.VMEM),
-        ],
-        out_specs=pl.BlockSpec(memory_space=pl.ANY),
+        out_shape=(
+            jax.ShapeDtypeStruct(tensor_slab.shape, f32),
+            jax.ShapeDtypeStruct((rank, rows), f32),
+        ),
+        in_specs=[anywhere, vmem, vmem, vmem, vmem, vmem],
+        out_specs=(anywhere, vmem),
         scratch_shapes=[
             pltpu.VMEM((slices, rows, cols), f32),
             pltpu.VMEM((links, slots, rows, cols), f32),
             pltpu.VMEM((links, 2, rows, cols), f32),
+            pltpu.VMEM((8, rows), f32),
             pltpu.VMEM((links, 8, rows), f32),
             pltpu.VMEM((links, 2, blocks, tile, tile), bf16),
-            pltpu.SemaphoreType.DMA((slices,)),
-            pltpu.SemaphoreType.DMA((links, slots)),
-            pltpu.SemaphoreType.DMA((links, slots)),
-            pltpu.SemaphoreType.DMA((links, 2)),
-            pltpu.SemaphoreType.DMA((links, 2)),
-            pltpu.SemaphoreType.DMA((links,)),
-            pltpu.SemaphoreType.DMA((links,)),
-            pltpu.SemaphoreType.DMA((slices,)),
+            pltpu.VMEM((cols, rank), f32),
+            pltpu.VMEM((rows, rank), f32),
+            pltpu.VMEM((rows, rank), f32),
+            pltpu.VMEM((rank, rank), f32),
+            pltpu.VMEM((others, share, rank), f32),
+            pltpu.VMEM((others, rank, rank), f32),
+            pltpu.VMEM((links + 2, *packed_shape), f32),
+            pltpu.VMEM((links + 1, *packed_shape), f32),
+            pltpu.VMEM((others, *packed_shape), f32),
+            dma((slices,)),
+            dma((links, slots)),
+            dma((links, slots)),
+            dma((links, 2)),
+            dma((links, 2)),
+            dma((links,)),
+            dma((links,)),
+            dma((slices,)),
+            dma((others,)),
+            dma((others,)),
+            dma((others,)),
+            dma((others,)),
+            dma((links + 1,)),
+            dma((links + 1,)),
+            dma((others,)),
+            dma((others,)),
         ],
         compiler_params=pltpu.CompilerParams(
             collective_id=0, has_side_effects=True, vmem_limit_bytes=56 * 2**20
         ),
-    )(slab, signs)
-
-
-def shards(tensor_slab, sign_flips, mode2_factor, mode3_factor, fibre_col, fibre_depth):
-    mixed_slab = mix(tensor_slab, sign_flips)
-    total_count = fibre_col.shape[0] * lax.axis_size("blk")
-    picked = mixed_slab[fibre_depth, :, fibre_col]
-    khatri = mode2_factor[fibre_col] * mode3_factor[fibre_depth]
-    moment_scale = 1.0 / math.sqrt(total_count)
-    gram_part = contract_samples(khatri, khatri) * (1.0 / total_count)
-    identity = jnp.eye(khatri.shape[1], dtype=jnp.float32)
-    moment_part = contract_samples(picked, khatri) * moment_scale
-    moment, gram = lax.psum((moment_part, gram_part), "blk")
-    factor_update = solve_normal(gram + ridge * identity, moment)
-    return (mixed_slab, factor_update)
+    )(
+        tensor_slab,
+        sign_flips.reshape(1, rows),
+        fibre_col.reshape(1, fibre_col.shape[0]),
+        fibre_depth.reshape(1, fibre_depth.shape[0]),
+        mode2_factor.T,
+        mode3_factor,
+    )
+    return mixed_slab, update_wide.T
 
 
 def solution(mesh):

time: 470 us -> 415 us (0.88)
  Pallas kernels: 369 us -> 402 us
  local copies, waits for them, and re-layouts: 39.9 us -> 12.5 us
  blocking collectives: 19.5 us -> 0 us
  between operations: 14.2 us -> 0.65 us
  other arithmetic: 12.8 us -> 0 us
  matrix products: 7.72 us -> 0 us
  waiting for transfers between devices: 6.97 us -> 0 us
    pallas_call x1, Pallas kernels: 369 us -> 402 us  [shards(): pl.pallas_call(functools.partial(mixing_kernel, plan), out_shape=(jax.Sha...]
    psum x1 -> x0, blocking collectives: 19.5 us -> none  [shards(): moment, gram = lax.psum((moment_part, gram_part), 'blk')]
    pallas_call x1 -> x0, local copies, waits for them, and re-layouts: 16.4 us -> none  [mix(): pl.pallas_call(functools.partial(mixing_kernel, plan), out_shape=jax.Shap...]
    another operation x5 -> x0, other arithmetic: 12.1 us -> none  [the longest x3 6.52 us: solve_normal(): factor_chol = jnp.linalg.cholesky(gram)]
    gather x3 -> x0, local copies, waits for them, and re-layouts: 10 us -> none  [the longest x1 7.94 us: shards(): picked = mixed_slab[fibre_depth, :, fibre_col]]
    psum x1 -> x0, waiting for transfers between devices: 6.95 us -> none  [shards(): moment, gram = lax.psum((moment_part, gram_part), 'blk')]
    dot_general x2 -> x0, matrix products: 4.9 us -> none  [contract_samples(): lax.dot_general(picked, khatri, (((0,), (0,)), ((), ())), precision=lax.P...]
    unnamed x10 -> x4, local copies, waits for them, and re-layouts: 12.8 us -> 12.5 us
  transfers between devices with their start and end apart: 1 -> 0, of which waited for: 1 -> 0; matrix products, arithmetic and copies ran while one was open for 3% -> 0% of each run, Pallas kernels for 0% -> 0%
where the time goes in v2:
time: 415 us
  Pallas kernels  402 us (97%)
  local copies, waits for them, and re-layouts  12.5 us (3%)
    pallas_call x1, Pallas kernels, shards(): pl.pallas_call(functools.partial(mixing_kernel, plan), out_shape=(jax.Sha...  402 us
    unnamed x4, local copies, waits for them, and re-layouts  12.5 us

profile of v2, /device:TPU:0, one launch (start us, length us, event | category | flops | bytes accessed | tf_op | source)
XLA Modules:
  0.0 415.3 jit_solution(7602956083041228422)
XLA Ops:
  0.6 402.1 %shard_map.77 = (f32[8,1024,512]{2,1,0:T(8,128)}, f32[64,1024]{1,0:T(8,128)}) custom-call(f32[8,1024,512]{2,1,0:T(8,128)} %slab.1, s32[1,1024]{1,0:T(1,128)} %bitcast.7, s32[1,512]{1,0:T(1,128)} %bitcast.8, s32[1,512]{1,0:T(1,128)} %bitcast.9, f32[64,512]{1,0:T(8,128)} %bitcast.6, f32[8,64]{1,0:T(8,128)} %mode3.1), custom_call_target="tpu_custom_call" | custom-call | tf_op jit(solution)/shard_map/pallas_call | solution.py:379
  402.8 0.0 copy-start
  402.8 11.8 %copy.10 = f32[8,1024,512]{2,1,0:T(8,128)} copy(f32[8,1024,512]{2,1,0:T(8,128)} %get-tuple-element.8) | data formatting | bytes 33554432
  414.6 0.0 copy-done
  414.6 0.7 copy.11
Async XLA Ops:
  402.8 11.8 %copy-start = (f32[64,1024]{1,0:T(8,128)S(1)}, f32[64,1024]{1,0:T(8,128)}, u32[]{:S(2)}) copy-start(f32[64,1024]{1,0:T(8,128)} %get-tuple-element.5) | copy-start | bytes 786436

commit v3 on v2

--- a/solution.py
+++ b/solution.py
@@ -63,9 +63,15 @@
     return found + exact_dot(found, identity - exact_dot(gram, found))
 
 
+def split_three(value):
+    high, rest = split_two(value)
+    low = (value - high.astype(f32) - rest.astype(f32)).astype(bf16)
+    return high, rest, low
+
+
 def mixing_kernel(plan, slab, flips, fibre_col, fibre_depth, mode2_wide, mode3, out, update_wide,
                   held, landed, core_landed, signs, near_signs, tables,
-                  mode2, update, moment, gram, moment_in, gram_in, packed, packed_in, gathered,
+                  mode2, update, moment_wide, gram_wide, moment, gram, moment_in, gram_in, packed, packed_in, gathered,
                   load_sem, link_send, link_recv, core_send, core_recv, sign_send, sign_recv, out_sem,
                   moment_send, moment_recv, gram_send, gram_recv, pack_send, pack_recv, gather_send, gather_recv):
     parties, blks, links, per_group, depth, slots = plan
@@ -243,29 +249,43 @@
 
     def contract_local():
         mode2[...] = mode2_wide[...].T
-        moment[...] = jnp.zeros_like(moment)
-        gram[...] = jnp.zeros_like(gram)
+        moment_wide[...] = jnp.zeros_like(moment_wide)
+        gram_wide[...] = jnp.zeros_like(gram_wide)
         samples = fibre_col.shape[1]
 
         @pl.loop(0, slices)
         def _(chunk):
-            place = lax.broadcasted_iota(jnp.int32, (cols, samples), 0) + chunk * cols
-            sampled = fibre_depth[...] * cols + fibre_col[...]
+            place = lax.broadcasted_iota(jnp.int32, (cols, samples), 0)
+            sampled = (fibre_depth[...] - chunk) * cols + fibre_col[...]
             counts = jnp.sum((place == sampled).astype(f32), axis=1, keepdims=True)
             khatri = mode2[...] * mode3[pl.ds(chunk, 1), :]
-            weights = khatri * counts
-            gram[...] += exact_dot(weights.T, khatri)
+            terms = split_three(khatri * counts)
+            terms = [term.astype(f32) for term in terms]
+            weights = jnp.concatenate(
+                [
+                    jnp.concatenate([terms[0], terms[1]], axis=1).astype(bf16),
+                    jnp.concatenate([terms[2], jnp.zeros_like(terms[2])], axis=1).astype(bf16),
+                ],
+                axis=1,
+            )
+            turned = jnp.concatenate(split_three(khatri.T), axis=0)
+            gram_wide[...] += jnp.dot(turned, weights, preferred_element_type=f32)
 
             @pl.loop(0, blocks)
             def _(block):
                 lines = pl.ds(pl.multiple_of(block * tile, tile), tile)
-                moment[lines, :] += exact_dot(held[chunk, lines, :], weights)
-
+                sums = moment_wide[lines, :]
+                for term in split_three(held[chunk, lines, :]):
+                    sums += jnp.dot(term, weights, preferred_element_type=f32)
+                moment_wide[lines, :] = sums
+
+        fold = gram_wide[:rank] + gram_wide[rank:2 * rank] + gram_wide[2 * rank:]
+        gram[...] = fold[:, :rank] + fold[:, rank:2 * rank] + fold[:, 2 * rank:3 * rank]
         parts = []
         for block in range(blocks):
-            value = moment[block * tile:(block + 1) * tile, :]
-            high, rest = split_two(value)
-            low = (value - high.astype(f32) - rest.astype(f32)).astype(bf16)
+            value = moment_wide[block * tile:(block + 1) * tile, :]
+            value = value[:, :rank] + value[:, rank:2 * rank] + value[:, 2 * rank:3 * rank]
+            high, rest, low = split_three(value)
             table = tables[0, 0, block]
             sums = jnp.dot(table, low, preferred_element_type=f32)
             sums += jnp.dot(table, rest, preferred_element_type=f32)
@@ -393,6 +413,8 @@
             pltpu.VMEM((links, 2, blocks, tile, tile), bf16),
             pltpu.VMEM((cols, rank), f32),
             pltpu.VMEM((rows, rank), f32),
+            pltpu.VMEM((rows, 4 * rank), f32),
+            pltpu.VMEM((3 * rank, 4 * rank), f32),
             pltpu.VMEM((rows, rank), f32),
             pltpu.VMEM((rank, rank), f32),
             pltpu.VMEM((others, share, rank), f32),

time: 415 us -> 409 us (0.986)
  Pallas kernels: 402 us -> 396 us
    pallas_call x1, Pallas kernels: 402 us -> 396 us  [shards(): pl.pallas_call(functools.partial(mixing_kernel, plan), out_shape=(jax.Sha...]
where the time goes in v3:
time: 409 us
  Pallas kernels  396 us (97%)
  local copies, waits for them, and re-layouts  12.5 us (3%)
    pallas_call x1, Pallas kernels, shards(): pl.pallas_call(functools.partial(mixing_kernel, plan), out_shape=(jax.Sha...  396 us
    unnamed x4, local copies, waits for them, and re-layouts  12.5 us

profile of v3, /device:TPU:0, one launch (start us, length us, event | category | flops | bytes accessed | tf_op | source)
XLA Modules:
  0.0 408.7 jit_solution(17970918843106593855)
XLA Ops:
  0.6 395.6 %shard_map.77 = (f32[8,1024,512]{2,1,0:T(8,128)}, f32[64,1024]{1,0:T(8,128)}) custom-call(f32[8,1024,512]{2,1,0:T(8,128)} %slab.1, s32[1,1024]{1,0:T(1,128)} %bitcast.7, s32[1,512]{1,0:T(1,128)} %bitcast.8, s32[1,512]{1,0:T(1,128)} %bitcast.9, f32[64,512]{1,0:T(8,128)} %bitcast.6, f32[8,64]{1,0:T(8,128)} %mode3.1), custom_call_target="tpu_custom_call" | custom-call | tf_op jit(solution)/shard_map/pallas_call | solution.py:399
  396.2 0.0 copy-start
  396.2 11.8 %copy.10 = f32[8,1024,512]{2,1,0:T(8,128)} copy(f32[8,1024,512]{2,1,0:T(8,128)} %get-tuple-element.8) | data formatting | bytes 33554432
  408.0 0.0 copy-done
  408.0 0.7 copy.11
Async XLA Ops:
  396.2 11.8 %copy-start = (f32[64,1024]{1,0:T(8,128)S(1)}, f32[64,1024]{1,0:T(8,128)}, u32[]{:S(2)}) copy-start(f32[64,1024]{1,0:T(8,128)} %get-tuple-element.5) | copy-start | bytes 786436

commit v4 on v3

--- a/solution.py
+++ b/solution.py
@@ -45,8 +45,8 @@
     return jnp.dot(left, right, precision=lax.Precision.HIGHEST, preferred_element_type=f32)
 
 
-def inverse_of(gram):
-    order = gram.shape[0]
+def eliminated(work, first, last):
+    order = work.shape[0]
     rows_idx = lax.broadcasted_iota(jnp.int32, (order, order), 0)
     cols_idx = lax.broadcasted_iota(jnp.int32, (order, order), 1)
 
@@ -58,9 +58,13 @@
         row = jnp.where(on_col[0:1], 1.0, row) / pivot
         return jnp.where(on_row, row, jnp.where(on_col, 0.0, work) - col * row)
 
-    found = lax.fori_loop(0, order, eliminate, gram)
-    identity = (rows_idx == cols_idx).astype(f32)
-    return found + exact_dot(found, identity - exact_dot(gram, found))
+    return lax.fori_loop(first, last, eliminate, work)
+
+
+def identity_of(order):
+    rows_idx = lax.broadcasted_iota(jnp.int32, (order, order), 0)
+    cols_idx = lax.broadcasted_iota(jnp.int32, (order, order), 1)
+    return (rows_idx == cols_idx).astype(f32)
 
 
 def split_three(value):
@@ -69,11 +73,12 @@
     return high, rest, low
 
 
-def mixing_kernel(plan, slab, flips, fibre_col, fibre_depth, mode2_wide, mode3, out, update_wide,
-                  held, landed, core_landed, signs, near_signs, tables,
-                  mode2, update, moment_wide, gram_wide, moment, gram, moment_in, gram_in, packed, packed_in, gathered,
-                  load_sem, link_send, link_recv, core_send, core_recv, sign_send, sign_recv, out_sem,
-                  moment_send, moment_recv, gram_send, gram_recv, pack_send, pack_recv, gather_send, gather_recv):
+def mixing_kernel(plan, slab, flips, fibre_col, fibre_depth, mode2_wide, mode3, held, update_wide,
+                  landed, core_landed, signs, near_signs, tables,
+                  mode2, update, weights, moment_wide, gram_wide, moment, shares, shares_in,
+                  gram, gram_in, solver, packed, packed_in, gathered,
+                  load_sem, link_send, link_recv, core_send, core_recv, sign_send, sign_recv,
+                  share_send, share_recv, gram_send, gram_recv, pack_send, pack_recv, gather_send, gather_recv):
     parties, blks, links, per_group, depth, slots = plan
     slices, rows, cols = held.shape
     tile = tables.shape[-1]
@@ -144,9 +149,6 @@
 
     def load_copy(chunk):
         return pltpu.make_async_copy(slab.at[chunk], held.at[chunk], load_sem.at[chunk])
-
-    def out_copy(chunk):
-        return pltpu.make_async_copy(held.at[chunk], out.at[chunk], out_sem.at[chunk])
 
     def combine(chunk, other, bit, scale):
         mine = side(bit) * scale
@@ -203,16 +205,13 @@
             for block, part in enumerate(butterflies(parts)):
                 held[chunk, block * tile:(block + 1) * tile, span] = part
 
-    def rows_of(blk):
-        return pl.ds(pl.multiple_of(blk * share, share), share)
-
-    def moment_copy(off):
+    def share_copy(off):
         target = lax.rem(my_blk + off, blks)
         return pltpu.make_async_remote_copy(
-            src_ref=moment.at[rows_of(target)],
-            dst_ref=moment_in.at[off - 1],
-            send_sem=moment_send.at[off - 1],
-            recv_sem=moment_recv.at[off - 1],
+            src_ref=shares.at[target],
+            dst_ref=shares_in.at[off - 1],
+            send_sem=share_send.at[off - 1],
+            recv_sem=share_recv.at[off - 1],
             device_id={"blk": target},
             device_id_type=MESH,
         )
@@ -247,7 +246,7 @@
             device_id_type=MESH,
         )
 
-    def contract_local():
+    def weigh_samples():
         mode2[...] = mode2_wide[...].T
         moment_wide[...] = jnp.zeros_like(moment_wide)
         gram_wide[...] = jnp.zeros_like(gram_wide)
@@ -259,28 +258,37 @@
             sampled = (fibre_depth[...] - chunk) * cols + fibre_col[...]
             counts = jnp.sum((place == sampled).astype(f32), axis=1, keepdims=True)
             khatri = mode2[...] * mode3[pl.ds(chunk, 1), :]
-            terms = split_three(khatri * counts)
-            terms = [term.astype(f32) for term in terms]
-            weights = jnp.concatenate(
+            terms = [term.astype(f32) for term in split_three(khatri * counts)]
+            wide = jnp.concatenate(
                 [
                     jnp.concatenate([terms[0], terms[1]], axis=1).astype(bf16),
                     jnp.concatenate([terms[2], jnp.zeros_like(terms[2])], axis=1).astype(bf16),
                 ],
                 axis=1,
             )
+            weights[chunk] = wide
             turned = jnp.concatenate(split_three(khatri.T), axis=0)
-            gram_wide[...] += jnp.dot(turned, weights, preferred_element_type=f32)
-
-            @pl.loop(0, blocks)
-            def _(block):
-                lines = pl.ds(pl.multiple_of(block * tile, tile), tile)
-                sums = moment_wide[lines, :]
-                for term in split_three(held[chunk, lines, :]):
-                    sums += jnp.dot(term, weights, preferred_element_type=f32)
-                moment_wide[lines, :] = sums
+            gram_wide[...] += jnp.dot(turned, wide, preferred_element_type=f32)
 
         fold = gram_wide[:rank] + gram_wide[rank:2 * rank] + gram_wide[2 * rank:]
-        gram[...] = fold[:, :rank] + fold[:, rank:2 * rank] + fold[:, 2 * rank:3 * rank]
+        fold = fold[:, :rank] + fold[:, rank:2 * rank] + fold[:, 2 * rank:3 * rank]
+        gram[...] = jnp.concatenate([fold, jnp.zeros_like(fold)], axis=1)
+        for off in range(1, blks):
+            gram_copy(off).start()
+
+    def contract(slot):
+        count = min(links, slices - links * slot)
+
+        @pl.loop(0, count * blocks)
+        def _(at):
+            chunk = links * slot + at // blocks
+            lines = pl.ds(pl.multiple_of((at % blocks) * tile, tile), tile)
+            sums = moment_wide[lines, :]
+            for term in split_three(held[chunk, lines, :]):
+                sums += jnp.dot(term, weights[chunk], preferred_element_type=f32)
+            moment_wide[lines, :] = sums
+
+    def send_shares():
         parts = []
         for block in range(blocks):
             value = moment_wide[block * tile:(block + 1) * tile, :]
@@ -293,24 +301,35 @@
             parts.append(sums * side(1))
         for block, part in enumerate(butterflies(parts)):
             moment[block * tile:(block + 1) * tile, :] = part
+        half = share // 2
+        for blk in range(blks):
+            at = blk * share
+            shares[blk] = jnp.concatenate([moment[at:at + half, :], moment[at + half:at + share, :]], axis=1)
         for off in range(1, blks):
-            moment_copy(off).start()
-            gram_copy(off).start()
+            share_copy(off).start()
+
+    def start_inverse():
+        total_gram = gram[:, :rank]
+        for off in range(1, blks):
+            gram_copy(off).wait()
+            total_gram = total_gram + gram_in[off - 1, :, :rank]
+        total_gram = total_gram * (1.0 / sample_count) + identity_of(rank) * ridge
+        solver[0] = total_gram
+        solver[1] = eliminated(total_gram, 0, rank // 2)
+
+    def finish_inverse():
+        found = eliminated(solver[1], rank // 2, rank)
+        solver[1] = found + exact_dot(found, identity_of(rank) - exact_dot(solver[0], found))
 
     def solve_share():
+        own = shares[my_blk]
         for off in range(1, blks):
-            moment_copy(off).wait()
-            gram_copy(off).wait()
-        whole_gram = gram[...]
-        own = moment[rows_of(my_blk), :]
-        for off in range(1, blks):
-            whole_gram = whole_gram + gram_in[off - 1]
-            own = own + moment_in[off - 1]
-        rows_idx = lax.broadcasted_iota(jnp.int32, (rank, rank), 0)
-        cols_idx = lax.broadcasted_iota(jnp.int32, (rank, rank), 1)
-        whole_gram = whole_gram * (1.0 / sample_count) + jnp.where(rows_idx == cols_idx, ridge, 0.0)
-        solved = exact_dot(own * (scale / math.sqrt(sample_count)), inverse_of(whole_gram))
-        packed[0] = jnp.concatenate([solved[: share // 2], solved[share // 2:]], axis=1)
+            share_copy(off).wait()
+            own = own + shares_in[off - 1]
+        own = own * (scale / math.sqrt(sample_count))
+        packed[0] = jnp.concatenate(
+            [exact_dot(own[:, :rank], solver[1]), exact_dot(own[:, rank:], solver[1])], axis=1
+        )
         pack_copy(0).start()
 
     def pack_step(bit):
@@ -335,7 +354,7 @@
             write_share(lax.rem(my_blk + blks - off, blks), gathered[off - 1])
         update_wide[...] = update[...].T
 
-    contract_local()
+    weigh_samples()
     for slot in range(total):
         if 1 <= slot <= per_group:
             for link in range(links):
@@ -344,6 +363,9 @@
                     copy.wait()
                     combine(chunk_at(link, slot - 1), core_landed.at[link, (slot - 1) % 2], 0, 1.0)
         if slot < per_group:
+            contract(slot)
+            if slot == per_group - 1:
+                send_shares()
             for link in range(links):
                 copy = link_copy(link, slot)
                 if copy is not None:
@@ -354,6 +376,10 @@
                 if copy is not None:
                     copy.start()
         else:
+            if slot == per_group:
+                pack_step(0)
+            if slot == total - 1:
+                write_update()
             last = slot >= total - per_group
             for link in range(links):
                 copy = link_copy(link, slot)
@@ -361,21 +387,19 @@
                     copy.wait()
                     chunk = chunk_at(link, slot)
                     combine(chunk, landed.at[link, slot % slots], link + 1, scale if last else 1.0)
-                    if last:
-                        out_copy(chunk).start()
+        if per_group < slot <= per_group + links:
+            pack_step(slot - per_group)
         if slot + depth < total:
             for link in range(links):
                 copy = link_copy(link, slot + depth)
                 if copy is not None:
                     copy.start()
         if slot == 1:
+            start_inverse()
+        if slot == 2:
+            finish_inverse()
+        if slot == per_group - 1:
             solve_share()
-        elif 2 <= slot <= links + 2:
-            pack_step(slot - 2)
-        elif slot == links + 3:
-            write_update()
-    for chunk in range(slices):
-        out_copy(chunk).wait()
 
 
 def shards(tensor_slab, sign_flips, mode2_factor, mode3_factor, fibre_col, fibre_depth):
@@ -399,13 +423,12 @@
     mixed_slab, update_wide = pl.pallas_call(
         functools.partial(mixing_kernel, plan),
         out_shape=(
-            jax.ShapeDtypeStruct(tensor_slab.shape, f32),
+            pltpu.VMEM(tensor_slab.shape, f32),
             jax.ShapeDtypeStruct((rank, rows), f32),
         ),
         in_specs=[anywhere, vmem, vmem, vmem, vmem, vmem],
-        out_specs=(anywhere, vmem),
+        out_specs=(vmem, vmem),
         scratch_shapes=[
-            pltpu.VMEM((slices, rows, cols), f32),
             pltpu.VMEM((links, slots, rows, cols), f32),
             pltpu.VMEM((links, 2, rows, cols), f32),
             pltpu.VMEM((8, rows), f32),
@@ -413,12 +436,15 @@
             pltpu.VMEM((links, 2, blocks, tile, tile), bf16),
             pltpu.VMEM((cols, rank), f32),
             pltpu.VMEM((rows, rank), f32),
+            pltpu.VMEM((slices, cols, 4 * rank), bf16),
             pltpu.VMEM((rows, 4 * rank), f32),
             pltpu.VMEM((3 * rank, 4 * rank), f32),
             pltpu.VMEM((rows, rank), f32),
-            pltpu.VMEM((rank, rank), f32),
-            pltpu.VMEM((others, share, rank), f32),
-            pltpu.VMEM((others, rank, rank), f32),
+            pltpu.VMEM((blks, *packed_shape), f32),
+            pltpu.VMEM((others, *packed_shape), f32),
+            pltpu.VMEM((rank, 2 * rank), f32),
+            pltpu.VMEM((others, rank, 2 * rank), f32),
+            pltpu.VMEM((2, rank, rank), f32),
             pltpu.VMEM((links + 2, *packed_shape), f32),
             pltpu.VMEM((links + 1, *packed_shape), f32),
             pltpu.VMEM((others, *packed_shape), f32),
@@ -429,7 +455,6 @@
             dma((links, 2)),
             dma((links,)),
             dma((links,)),
-            dma((slices,)),
             dma((others,)),
             dma((others,)),
             dma((others,)),
@@ -440,7 +465,7 @@
             dma((others,)),
         ],
         compiler_params=pltpu.CompilerParams(
-            collective_id=0, has_side_effects=True, vmem_limit_bytes=56 * 2**20
+            collective_id=0, has_side_effects=True, vmem_limit_bytes=40 * 2**20
         ),
     )(
         tensor_slab,

time: 409 us -> 392 us (0.958)
  Pallas kernels: 396 us -> 384 us
  local copies, waits for them, and re-layouts: 12.5 us -> 6.87 us
    pallas_call x1, Pallas kernels: 396 us -> 384 us  [shards(): pl.pallas_call(functools.partial(mixing_kernel, plan), out_shape=(pltpu.V...]
    unnamed x4, local copies, waits for them, and re-layouts: 12.5 us -> 6.87 us
where the time goes in v4:
time: 392 us
  Pallas kernels  384 us (98%)
  local copies, waits for them, and re-layouts  6.87 us (2%)
    pallas_call x1, Pallas kernels, shards(): pl.pallas_call(functools.partial(mixing_kernel, plan), out_shape=(pltpu.V...  384 us

profile of v4, /device:TPU:0, one launch (start us, length us, event | category | flops | bytes accessed | tf_op | source)
XLA Modules:
  0.0 392.0 jit_solution(3211414570047840259)
XLA Ops:
  0.6 384.5 %shard_map.77 = (f32[8,1024,512]{2,1,0:T(8,128)S(1)}, f32[64,1024]{1,0:T(8,128)}) custom-call(f32[8,1024,512]{2,1,0:T(8,128)} %slab.1, s32[1,1024]{1,0:T(1,128)} %bitcast.7, s32[1,512]{1,0:T(1,128)} %bitcast.8, s32[1,512]{1,0:T(1,128)} %bitcast.9, f32[64,512]{1,0:T(8,128)} %bitcast.6, f32[8,64]{1,0:T(8,128)} %mode3.1), custom_call_target="tpu_custom_call" | custom-call | tf_op jit(solution)/shard_map/pallas_call | solution.py:423
  385.1 0.0 copy-start
  385.1 6.2 %copy.10 = f32[8,1024,512]{2,1,0:T(8,128)} copy(f32[8,1024,512]{2,1,0:T(8,128)S(1)} %get-tuple-element.6) | data formatting | bytes 33554432
  391.3 0.0 copy-done
  391.3 0.7 copy.11
Async XLA Ops:
  385.1 6.2 %copy-start = (f32[64,1024]{1,0:T(8,128)S(1)}, f32[64,1024]{1,0:T(8,128)}, u32[]{:S(2)}) copy-start(f32[64,1024]{1,0:T(8,128)} %get-tuple-element.5) | copy-start | bytes 786436

commit v5 on v4

--- a/solution.py
+++ b/solution.py
@@ -219,7 +219,7 @@
     def gram_copy(off):
         return pltpu.make_async_remote_copy(
             src_ref=gram,
-            dst_ref=gram_in.at[off - 1],
+            dst_ref=gram_in.at[my_blk],
             send_sem=gram_send.at[off - 1],
             recv_sem=gram_recv.at[off - 1],
             device_id={"blk": lax.rem(my_blk + off, blks)},
@@ -246,14 +246,13 @@
             device_id_type=MESH,
         )
 
-    def weigh_samples():
-        mode2[...] = mode2_wide[...].T
-        moment_wide[...] = jnp.zeros_like(moment_wide)
-        gram_wide[...] = jnp.zeros_like(gram_wide)
+    def weigh_samples(slot):
+        count = min(links, slices - links * slot)
         samples = fibre_col.shape[1]
 
-        @pl.loop(0, slices)
-        def _(chunk):
+        @pl.loop(0, count)
+        def _(link):
+            chunk = links * slot + link
             place = lax.broadcasted_iota(jnp.int32, (cols, samples), 0)
             sampled = (fibre_depth[...] - chunk) * cols + fibre_col[...]
             counts = jnp.sum((place == sampled).astype(f32), axis=1, keepdims=True)
@@ -266,13 +265,15 @@
                 ],
                 axis=1,
             )
-            weights[chunk] = wide
+            weights[link] = wide
             turned = jnp.concatenate(split_three(khatri.T), axis=0)
             gram_wide[...] += jnp.dot(turned, wide, preferred_element_type=f32)
 
+    def send_gram():
         fold = gram_wide[:rank] + gram_wide[rank:2 * rank] + gram_wide[2 * rank:]
         fold = fold[:, :rank] + fold[:, rank:2 * rank] + fold[:, 2 * rank:3 * rank]
         gram[...] = jnp.concatenate([fold, jnp.zeros_like(fold)], axis=1)
+        gram_in[my_blk] = gram[...]
         for off in range(1, blks):
             gram_copy(off).start()
 
@@ -281,11 +282,11 @@
 
         @pl.loop(0, count * blocks)
         def _(at):
-            chunk = links * slot + at // blocks
+            link = at // blocks
             lines = pl.ds(pl.multiple_of((at % blocks) * tile, tile), tile)
             sums = moment_wide[lines, :]
-            for term in split_three(held[chunk, lines, :]):
-                sums += jnp.dot(term, weights[chunk], preferred_element_type=f32)
+            for term in split_three(held[links * slot + link, lines, :]):
+                sums += jnp.dot(term, weights[link], preferred_element_type=f32)
             moment_wide[lines, :] = sums
 
     def send_shares():
@@ -309,10 +310,11 @@
             share_copy(off).start()
 
     def start_inverse():
-        total_gram = gram[:, :rank]
         for off in range(1, blks):
             gram_copy(off).wait()
-            total_gram = total_gram + gram_in[off - 1, :, :rank]
+        total_gram = gram_in[0, :, :rank]
+        for blk in range(1, blks):
+            total_gram = total_gram + gram_in[blk, :, :rank]
         total_gram = total_gram * (1.0 / sample_count) + identity_of(rank) * ridge
         solver[0] = total_gram
         solver[1] = eliminated(total_gram, 0, rank // 2)
@@ -321,15 +323,12 @@
         found = eliminated(solver[1], rank // 2, rank)
         solver[1] = found + exact_dot(found, identity_of(rank) - exact_dot(solver[0], found))
 
-    def solve_share():
+    def start_pack():
         own = shares[my_blk]
         for off in range(1, blks):
             share_copy(off).wait()
             own = own + shares_in[off - 1]
-        own = own * (scale / math.sqrt(sample_count))
-        packed[0] = jnp.concatenate(
-            [exact_dot(own[:, :rank], solver[1]), exact_dot(own[:, rank:], solver[1])], axis=1
-        )
+        packed[0] = own * (scale / math.sqrt(sample_count))
         pack_copy(0).start()
 
     def pack_step(bit):
@@ -352,9 +351,13 @@
         for off in range(1, blks):
             gather_copy(off).wait()
             write_share(lax.rem(my_blk + blks - off, blks), gathered[off - 1])
-        update_wide[...] = update[...].T
-
-    weigh_samples()
+        step = min(rows, 256)
+        for at in range(0, rows, step):
+            update_wide[:, at:at + step] = exact_dot(update[at:at + step, :], solver[1]).T
+
+    mode2[...] = mode2_wide[...].T
+    moment_wide[...] = jnp.zeros_like(moment_wide)
+    gram_wide[...] = jnp.zeros_like(gram_wide)
     for slot in range(total):
         if 1 <= slot <= per_group:
             for link in range(links):
@@ -363,8 +366,10 @@
                     copy.wait()
                     combine(chunk_at(link, slot - 1), core_landed.at[link, (slot - 1) % 2], 0, 1.0)
         if slot < per_group:
+            weigh_samples(slot)
             contract(slot)
             if slot == per_group - 1:
+                send_gram()
                 send_shares()
             for link in range(links):
                 copy = link_copy(link, slot)
@@ -394,12 +399,12 @@
                 copy = link_copy(link, slot + depth)
                 if copy is not None:
                     copy.start()
-        if slot == 1:
+        if slot == per_group - 1:
+            start_pack()
+        if slot == per_group:
             start_inverse()
-        if slot == 2:
+        if slot == per_group + 1:
             finish_inverse()
-        if slot == per_group - 1:
-            solve_share()
 
 
 def shards(tensor_slab, sign_flips, mode2_factor, mode3_factor, fibre_col, fibre_depth):
@@ -436,14 +441,14 @@
             pltpu.VMEM((links, 2, blocks, tile, tile), bf16),
             pltpu.VMEM((cols, rank), f32),
             pltpu.VMEM((rows, rank), f32),
-            pltpu.VMEM((slices, cols, 4 * rank), bf16),
+            pltpu.VMEM((links, cols, 4 * rank), bf16),
             pltpu.VMEM((rows, 4 * rank), f32),
             pltpu.VMEM((3 * rank, 4 * rank), f32),
             pltpu.VMEM((rows, rank), f32),
             pltpu.VMEM((blks, *packed_shape), f32),
             pltpu.VMEM((others, *packed_shape), f32),
             pltpu.VMEM((rank, 2 * rank), f32),
-            pltpu.VMEM((others, rank, 2 * rank), f32),
+            pltpu.VMEM((blks, rank, 2 * rank), f32),
             pltpu.VMEM((2, rank, rank), f32),
             pltpu.VMEM((links + 2, *packed_shape), f32),
             pltpu.VMEM((links + 1, *packed_shape), f32),

time: 392 us -> 389 us (level)
  no operation moved by 1% of the time
where the time goes in v5:
time: 389 us
  Pallas kernels  381 us (98%)
  local copies, waits for them, and re-layouts  6.87 us (2%)
    pallas_call x1, Pallas kernels, shards(): pl.pallas_call(functools.partial(mixing_kernel, plan), out_shape=(pltpu.V...  381 us

profile of v5, /device:TPU:0, one launch (start us, length us, event | category | flops | bytes accessed | tf_op | source)
XLA Modules:
  0.0 388.8 jit_solution(7168520295706753840)
XLA Ops:
  0.6 381.3 %shard_map.77 = (f32[8,1024,512]{2,1,0:T(8,128)S(1)}, f32[64,1024]{1,0:T(8,128)}) custom-call(f32[8,1024,512]{2,1,0:T(8,128)} %slab.1, s32[1,1024]{1,0:T(1,128)} %bitcast.7, s32[1,512]{1,0:T(1,128)} %bitcast.8, s32[1,512]{1,0:T(1,128)} %bitcast.9, f32[64,512]{1,0:T(8,128)} %bitcast.6, f32[8,64]{1,0:T(8,128)} %mode3.1), custom_call_target="tpu_custom_call" | custom-call | tf_op jit(solution)/shard_map/pallas_call | solution.py:428
  381.9 0.0 copy-start
  382.0 6.2 %copy.10 = f32[8,1024,512]{2,1,0:T(8,128)} copy(f32[8,1024,512]{2,1,0:T(8,128)S(1)} %get-tuple-element.6) | data formatting | bytes 33554432
  388.1 0.0 copy-done
  388.1 0.7 copy.11
Async XLA Ops:
  381.9 6.2 %copy-start = (f32[64,1024]{1,0:T(8,128)S(1)}, f32[64,1024]{1,0:T(8,128)}, u32[]{:S(2)}) copy-start(f32[64,1024]{1,0:T(8,128)} %get-tuple-element.5) | copy-start | bytes 786436

commit v6 on v5

--- a/solution.py
+++ b/solution.py
@@ -73,8 +73,8 @@
     return high, rest, low
 
 
-def mixing_kernel(plan, slab, flips, fibre_col, fibre_depth, mode2_wide, mode3, held, update_wide,
-                  landed, core_landed, signs, near_signs, tables,
+def mixing_kernel(plan, slab, flips_far, col_far, depth_far, mode2_far, mode3_far, held, update_wide,
+                  flips, fibre_col, fibre_depth, mode2_wide, mode3, fetch_sem, landed, core_landed, signs, near_signs, tables,
                   mode2, update, weights, moment_wide, gram_wide, moment, shares, shares_in,
                   gram, gram_in, solver, packed, packed_in, gathered,
                   load_sem, link_send, link_recv, core_send, core_recv, sign_send, sign_recv,
@@ -164,8 +164,20 @@
             copy = link_copy(link, slot)
             if copy is not None:
                 copy.start()
+    pairs = (
+        (flips_far, flips),
+        (col_far, fibre_col),
+        (depth_far, fibre_depth),
+        (mode2_far, mode2_wide),
+        (mode3_far, mode3),
+    )
+    fetches = [pltpu.make_async_copy(far, near, fetch_sem.at[at]) for at, (far, near) in enumerate(pairs)]
+    for copy in fetches:
+        copy.start()
     for chunk in range(slices):
         load_copy(chunk).start()
+    for copy in fetches:
+        copy.wait()
     signs[...] = jnp.broadcast_to(flips[...].astype(f32), signs.shape)
     for link in range(links):
         sign_copy(link).start()
@@ -424,16 +436,23 @@
     plan = (parties, blks, links, per_group, depth, slots)
     dma = pltpu.SemaphoreType.DMA
     vmem = pl.BlockSpec(memory_space=pltpu.VMEM)
-    anywhere = pl.BlockSpec(memory_space=pl.ANY)
+    anywhere = pl.BlockSpec(memory_space=pltpu.HBM)
+    samples = fibre_col.shape[0]
     mixed_slab, update_wide = pl.pallas_call(
         functools.partial(mixing_kernel, plan),
         out_shape=(
             pltpu.VMEM(tensor_slab.shape, f32),
-            jax.ShapeDtypeStruct((rank, rows), f32),
+            pltpu.VMEM((rank, rows), f32),
         ),
-        in_specs=[anywhere, vmem, vmem, vmem, vmem, vmem],
+        in_specs=[anywhere] * 6,
         out_specs=(vmem, vmem),
         scratch_shapes=[
+            pltpu.VMEM((1, rows), jnp.int32),
+            pltpu.VMEM((1, samples), jnp.int32),
+            pltpu.VMEM((1, samples), jnp.int32),
+            pltpu.VMEM((rank, cols), f32),
+            pltpu.VMEM((slices, rank), f32),
+            dma((5,)),
             pltpu.VMEM((links, slots, rows, cols), f32),
             pltpu.VMEM((links, 2, rows, cols), f32),
             pltpu.VMEM((8, rows), f32),

time: 389 us -> 387 us (level)
  no operation moved by 1% of the time
where the time goes in v6:
time: 387 us
  Pallas kernels  380 us (98%)
  local copies, waits for them, and re-layouts  6.87 us (2%)
    pallas_call x1, Pallas kernels, shards(): pl.pallas_call(functools.partial(mixing_kernel, plan), out_shape=(pltpu.V...  380 us

profile of v6, /device:TPU:0, one launch (start us, length us, event | category | flops | bytes accessed | tf_op | source)
XLA Modules:
  0.0 387.1 jit_solution(16428526848145095930)
XLA Ops:
  0.6 379.6 %shard_map.77 = (f32[8,1024,512]{2,1,0:T(8,128)S(1)}, f32[64,1024]{1,0:T(8,128)S(1)}) custom-call(f32[8,1024,512]{2,1,0:T(8,128)} %slab.1, s32[1,1024]{1,0:T(1,128)} %bitcast.7, s32[1,512]{1,0:T(1,128)} %bitcast.8, s32[1,512]{1,0:T(1,128)} %bitcast.9, f32[64,512]{1,0:T(8,128)} %bitcast.6, f32[8,64]{1,0:T(8,128)} %mode3_far.1), custom_call_target="tpu_custom_call" | custom-call | tf_op jit(solution)/shard_map/pallas_call | solution.py:441
  380.2 6.2 %copy.10 = f32[8,1024,512]{2,1,0:T(8,128)} copy(f32[8,1024,512]{2,1,0:T(8,128)S(1)} %get-tuple-element.6) | data formatting | bytes 33554432
  386.4 0.7 copy.11
